TPU v7x, 32 devices: a whole 2x2x4 slice. The times are simulated.
32 devices in a mesh: groups: 2 (over x), ep: 4 (over y, core), col: 4 (over z).
Axes of the slice: x: 2, y: 2, z: 4, core: 2. Of those that a mesh axis runs over, the one named last changes fastest.
Arguments:
- tokens: bfloat16 [512, 4096], P(('groups', 'ep', 'col')), parts along dimension 0, may hold values from -6 to 6
- expert_ids: int32 [512, 8], P(('groups', 'ep', 'col')), parts along dimension 0, may hold values from 0 to 15, all different within a row; in each aligned block of 16 rows (0 to 15, 16 to 31, ...) at most 12 rows name the same one
- gate_weights: bfloat16 [512, 8], P(('groups', 'ep', 'col')), parts along dimension 0, may hold values from 0.099609375 to 0.5
- mix_coef: float32 [16, 2, 16], P('ep'), may hold values from -0.5 to 0.5
- factor_in: bfloat16 [16, 2, 4096, 256], P(('ep', 'col')), may hold values from -0.09375 to 0.09375
- factor_out: bfloat16 [16, 768, 256], P(('ep', 'col')), may hold values from -0.21875 to 0.21875
- basis_in: bfloat16 [16, 256, 1536], P(None, None, 'col'), may hold values from -0.375 to 0.375
- basis_out: bfloat16 [16, 256, 4096], P(None, None, 'col'), may hold values from -0.375 to 0.375
Outputs:
- moe_out: bfloat16 [512, 4096], P(('groups', 'ep', 'col')), parts along dimension 0
There are 2 independent parts, one for each index of `groups`. A program takes and returns all parts, laid end to end along the dimension named above; an argument that names none is the same for every part. Nothing has to cross between parts.
Inputs may be any that keep to these rules, and one draw needn't show every extreme that they name: `expert_ids`: each token names 8 different experts; among the 16 tokens of one device (aligned blocks of 16 rows) no expert is named by more than 12 tokens, a bound that some block reaches.
All inputs are finite; a program needn't handle non-finite values.
Results may differ from a plain program's by a relative error of at most 0.0092.
Values may be sent and summed in bfloat16 or wider, within the bound.
A program may use at most 64 MiB of HBM per device.

v0:
```python
import jax
import jax.numpy as jnp
from jax import lax
from jax.sharding import PartitionSpec as P


def shards(tokens, expert_ids, gate_weights, mix_coef, factor_in, factor_out, basis_in, basis_out):
    tok_count = tokens.shape[0]
    width = tokens.shape[1]
    topk = expert_ids.shape[1]
    hidden_units = factor_out.shape[1]
    count_ep = lax.axis_size("ep")
    count_col = lax.axis_size("col")
    experts = count_ep * count_col
    capacity = max(2, (3 * tok_count * topk + 2 * experts - 1) // (2 * experts))
    span_in = jnp.einsum(
        "ej,jrc->erc",
        mix_coef[:, 0, :],
        basis_in.astype(jnp.float32),
        precision=lax.Precision.HIGHEST,
    ).astype(jnp.bfloat16)
    span_out = jnp.einsum(
        "ej,jrc->erc",
        mix_coef[:, 1, :],
        basis_out.astype(jnp.float32),
        precision=lax.Precision.HIGHEST,
    ).astype(jnp.bfloat16)
    mix_in, mix_out = (
        lax.all_to_all(span_in, "col", split_axis=0, concat_axis=2, tiled=True),
        lax.all_to_all(span_out, "col", split_axis=0, concat_axis=2, tiled=True),
    )
    w_gate = jnp.dot(
        factor_in[0, 0], mix_in[0, :, :hidden_units], preferred_element_type=jnp.float32
    ).astype(jnp.bfloat16)
    w_up = jnp.dot(
        factor_in[0, 1], mix_in[0, :, hidden_units:], preferred_element_type=jnp.float32
    ).astype(jnp.bfloat16)
    w_down = jnp.dot(factor_out[0], mix_out[0], preferred_element_type=jnp.float32).astype(
        jnp.bfloat16
    )
    flat_ids = expert_ids.reshape(-1)
    slots_all = flat_ids.shape[0]
    onehot = (flat_ids[:, None] == jnp.arange(experts, dtype=jnp.int32)[None, :]).astype(jnp.int32)
    earlier = jnp.cumsum(onehot, axis=0) - onehot
    position = jnp.sum(earlier * onehot, axis=1)
    slot_index = flat_ids * capacity + position
    placing = (
        slot_index[:, None] == jnp.arange(experts * capacity, dtype=jnp.int32)[None, :]
    ).astype(jnp.bfloat16)
    token_of = jnp.arange(slots_all, dtype=jnp.int32) // topk
    owner_table = (token_of[:, None] == jnp.arange(tok_count, dtype=jnp.int32)[None, :]).astype(
        jnp.bfloat16
    )
    selector = jnp.dot(placing.T, owner_table, preferred_element_type=jnp.float32).astype(
        jnp.bfloat16
    )
    outgoing = jnp.dot(selector, tokens, preferred_element_type=jnp.float32).astype(jnp.bfloat16)
    outgoing = outgoing.reshape(experts, capacity, width)
    weighted = placing * gate_weights.reshape(-1)[:, None]
    combiner = jnp.dot(owner_table.T, weighted, preferred_element_type=jnp.float32).astype(
        jnp.bfloat16
    )
    arrived = lax.all_to_all(outgoing, ("ep", "col"), split_axis=0, concat_axis=0, tiled=True)
    flat_rows = arrived.reshape(-1, width)
    gate = jnp.dot(flat_rows, w_gate, preferred_element_type=jnp.float32)
    upper = jnp.dot(flat_rows, w_up, preferred_element_type=jnp.float32)
    hidden = (jax.nn.silu(gate) * upper).astype(jnp.bfloat16)
    result = jnp.dot(hidden, w_down, preferred_element_type=jnp.float32).astype(jnp.bfloat16)
    finished = result.reshape(arrived.shape)
    returned = lax.all_to_all(finished, ("ep", "col"), split_axis=0, concat_axis=0, tiled=True)
    returned = returned.reshape(experts * capacity, width)
    return jnp.dot(combiner, returned, preferred_element_type=jnp.float32).astype(jnp.bfloat16)


def solution(mesh):
    return jax.shard_map(
        shards,
        mesh=mesh,
        in_specs=(
            P(("groups", "ep", "col"), None),
            P(("groups", "ep", "col"), None),
            P(("groups", "ep", "col"), None),
            P("ep", None, None),
            P(("ep", "col"), None, None, None),
            P(("ep", "col"), None, None),
            P(None, None, "col"),
            P(None, None, "col"),
        ),
        out_specs=P(("groups", "ep", "col"), None),
        check_vma=False,
    )
```

profile of v0, /device:TPU:0, one launch (start us, length us, event | category | flops | bytes accessed | tf_op | source)
XLA Modules:
  0.0 213.0 jit_solution(3401006431831883304)
XLA Ops:
  0.9 1.1 copy-done
  1.9 2.8 %fusion.17 = bf16[4,256,384]{2,0,1:T(4,128)(2,1)S(1)} fusion(f32[4,16,1]{1,0,2:T(4,128)S(1)} %bitcast.51, bf16[16,256,384]{2,1,0:T(8,128)(2,1)S(1)} %copy-done), kind=kOutput, calls=%fused_computation.17 | convolution fusion | flops 75890688 | bytes 3932416 | tf_op jit(solution)/shard_map/ej,jrc->erc/dot_general | solution.py:16
  4.7 1.0 copy.26
  5.7 6.3 %all-to-all-start.1 = ((bf16[4,256,384]{2,1,0:T(8,128)(2,1)}), bf16[4,256,384]{2,1,0:T(8,128)(2,1)}, u32[]{:S(2)}, u32[]{:S(2)}) async-start(bf16[4,256,384]{2,1,0:T(8,128)(2,1)} %copy.26), calls=%async_computation.1 | async-start | bytes 1572864 | tf_op jit(solution)/shard_map/all_to_all | solution.py:29
  12.6 2.0 convolution_convert_fusion.4
  14.6 3.4 %reshape.40 = bf16[16,12,4096]{2,1,0:T(8,128)(2,1)} reshape(bf16[192,4096]{1,0:T(8,128)(2,1)} %convolution_convert_fusion.4) | data formatting | bytes 3145728 | tf_op jit(solution)/shard_map/reshape | solution.py:58
  18.0 14.2 %all-to-all-done.1 = bf16[4,256,384]{2,1,0:T(8,128)(2,1)} async-done(((bf16[4,256,384]{2,1,0:T(8,128)(2,1)}), bf16[4,256,384]{2,1,0:T(8,128)(2,1)}, u32[]{:S(2)}, u32[]{:S(2)}) %all-to-all-start.1) | async-done | bytes 786464 | tf_op jit(solution)/shard_map/all_to_all | solution.py:29
  32.2 4.4 %all-to-all-start = ((bf16[16,12,4096]{2,1,0:T(8,128)(2,1)}), bf16[16,12,4096]{2,1,0:T(8,128)(2,1)}, u32[]{:S(2)}, u32[]{:S(2)}) async-start(bf16[16,12,4096]{2,1,0:T(8,128)(2,1)} %reshape.40), calls=%async_computation | async-start | bytes 4194304 | tf_op jit(solution)/shard_map/all_to_all | solution.py:63
  36.7 11.4 %fusion.14 = bf16[4,256,1024]{2,0,1:T(4,128)(2,1)S(1)} fusion(f32[4,16,1]{1,0,2:T(4,128)S(1)} %bitcast.52, bf16[16,256,1024]{2,1,0:T(8,128)(2,1)} %param.15), kind=kOutput, calls=%fused_computation.16 | convolution fusion | flops 202375168 | bytes 10486016 | tf_op jit(solution)/shard_map/ej,jrc->erc/dot_general | solution.py:22
  48.1 1.9 copy.29
  50.1 36.0 %all-to-all-done = bf16[16,12,4096]{2,1,0:T(8,128)(2,1)} async-done(((bf16[16,12,4096]{2,1,0:T(8,128)(2,1)}), bf16[16,12,4096]{2,1,0:T(8,128)(2,1)}, u32[]{:S(2)}, u32[]{:S(2)}) %all-to-all-start) | async-done | bytes 1572896 | tf_op jit(solution)/shard_map/all_to_all | solution.py:63
  86.1 4.6 %all-to-all-start.2 = ((bf16[4,256,1024]{2,1,0:T(8,128)(2,1)}), bf16[4,256,1024]{2,1,0:T(8,128)(2,1)}, u32[]{:S(2)}, u32[]{:S(2)}) async-start(bf16[4,256,1024]{2,1,0:T(8,128)(2,1)} %copy.29), calls=%async_computation.2 | async-start | bytes 4194304 | tf_op jit(solution)/shard_map/all_to_all | solution.py:30
  90.7 2.4 %copy.27 = bf16[4,256,384]{1,2,0:T(8,128)(2,1)} copy(bf16[4,256,384]{2,1,0:T(8,128)(2,1)} %all-to-all-done.1) | data formatting | bytes 1572864 | tf_op jit(solution)/shard_map/all_to_all | solution.py:29
  93.1 3.6 %reshape.41 = bf16[192,4096]{1,0:T(8,128)(2,1)} reshape(bf16[16,12,4096]{2,1,0:T(8,128)(2,1)} %all-to-all-done) | data formatting | bytes 3145728 | tf_op jit(solution)/shard_map/reshape | solution.py:64
  96.7 6.6 %fusion.9 = f32[192,768]{1,0:T(8,128)} fusion(bf16[192,4096]{1,0:T(8,128)(2,1)} %reshape.41, bf16[1,2,4096,256]{3,2,1,0:T(8,128)(2,1)} %param.12, bf16[1,256,1536]{1,2,0:T(8,128)(2,1)} %bitcast.49), kind=kOutput, calls=%fused_computation.14 | convolution fusion | flops 2821718016 | bytes 4653056 | tf_op jit(solution)/shard_map/dot_general | solution.py:65
  103.3 6.6 %fusion.23 = bf16[192,768]{1,0:T(8,128)(2,1)} fusion(bf16[192,4096]{1,0:T(8,128)(2,1)} %reshape.41, bf16[1,2,4096,256]{3,2,1,0:T(8,128)(2,1)} %param.12, f32[192,768]{1,0:T(8,128)} %fusion.9, bf16[1,256,1536]{1,2,0:T(8,128)(2,1)} %bitcast.50), kind=kOutput, calls=%fused_computation.19 | convolution fusion | flops 2822602752 | bytes 4947968 | tf_op jit(solution)/shard_map/dot_general | solution.py:66
  109.9 29.0 %all-to-all-done.2 = bf16[4,256,1024]{2,1,0:T(8,128)(2,1)} async-done(((bf16[4,256,1024]{2,1,0:T(8,128)(2,1)}), bf16[4,256,1024]{2,1,0:T(8,128)(2,1)}, u32[]{:S(2)}, u32[]{:S(2)}) %all-to-all-start.2) | async-done | bytes 2097184 | tf_op jit(solution)/shard_map/all_to_all | solution.py:30
  138.9 3.9 %copy.30 = bf16[4,256,1024]{1,2,0:T(8,128)(2,1)} copy(bf16[4,256,1024]{2,1,0:T(8,128)(2,1)} %all-to-all-done.2) | data formatting | bytes 4194304 | tf_op jit(solution)/shard_map/all_to_all | solution.py:30
  142.8 6.6 %convolution_convert_fusion.3 = bf16[192,4096]{1,0:T(8,128)(2,1)} fusion(bf16[192,768]{1,0:T(8,128)(2,1)} %fusion.23, bf16[256,4096]{0,1:T(8,128)(2,1)} %bitcast.48, bf16[1,768,256]{2,1,0:T(8,128)(2,1)S(1)} %copy-done.4), kind=kOutput, calls=%fused_computation.5 | convolution fusion | flops 2822504448 | bytes 4358144 | tf_op jit(solution)/shard_map/dot_general | solution.py:68
  149.4 3.4 %reshape.42 = bf16[16,12,4096]{2,1,0:T(8,128)(2,1)} reshape(bf16[192,4096]{1,0:T(8,128)(2,1)} %convolution_convert_fusion.3) | data formatting | bytes 3145728 | tf_op jit(solution)/shard_map/reshape | solution.py:69
  152.8 4.6 %all-to-all-start.3 = ((bf16[16,12,4096]{2,1,0:T(8,128)(2,1)}), bf16[16,12,4096]{2,1,0:T(8,128)(2,1)}, u32[]{:S(2)}, u32[]{:S(2)}) async-start(bf16[16,12,4096]{2,1,0:T(8,128)(2,1)} %reshape.42), calls=%async_computation.3 | async-start | bytes 4194304 | tf_op jit(solution)/shard_map/all_to_all | solution.py:70
  157.5 49.2 %all-to-all-done.3 = bf16[16,12,4096]{2,1,0:T(8,128)(2,1)} async-done(((bf16[16,12,4096]{2,1,0:T(8,128)(2,1)}), bf16[16,12,4096]{2,1,0:T(8,128)(2,1)}, u32[]{:S(2)}, u32[]{:S(2)}) %all-to-all-start.3) | async-done | bytes 1572896 | tf_op jit(solution)/shard_map/all_to_all | solution.py:70
  206.8 3.6 %reshape.43 = bf16[192,4096]{1,0:T(8,128)(2,1)} reshape(bf16[16,12,4096]{2,1,0:T(8,128)(2,1)} %all-to-all-done.3) | data formatting | bytes 3145728 | tf_op jit(solution)/shard_map/reshape | solution.py:71
  210.4 2.6 %convolution_convert_fusion.5 = bf16[16,4096]{1,0:T(8,128)(2,1)} fusion(bf16[192,4096]{1,0:T(8,128)(2,1)} %reshape.43, s32[128]{0:T(128)S(1)} %get-tuple-element.8, bf16[128]{0:T(256)(128)(2,1)S(1)} %mul.33, s32[128]{0:T(128)S(1)} %get-tuple-element.7), kind=kOutput, calls=%fused_computation.7 | convolution fusion | flops 26072064 | bytes 1705216 | tf_op jit(solution)/shard_map/dot_general | solution.py:72
  (18 shorter events, 1.7 us)
Async XLA Ops:
  0.0 1.9 copy-start
  4.7 7.3 %copy-start.2 = (s32[16,8]{0,1:T(8,128)S(1)}, s32[16,8]{0,1:T(8,128)}, u32[]{:S(2)}) copy-start(s32[16,8]{0,1:T(8,128)} %param.9) | copy-start | bytes 1540
  4.7 7.9 %copy-start.1 = (bf16[16,4096]{1,0:T(8,128)(2,1)S(1)}, bf16[16,4096]{1,0:T(8,128)(2,1)}, u32[]{:S(2)}) copy-start(bf16[16,4096]{1,0:T(8,128)(2,1)} %param.8) | copy-start | bytes 393220
  5.7 26.5 %all-to-all-start.1 = ((bf16[4,256,384]{2,1,0:T(8,128)(2,1)}), bf16[4,256,384]{2,1,0:T(8,128)(2,1)}, u32[]{:S(2)}, u32[]{:S(2)}) async-start(bf16[4,256,384]{2,1,0:T(8,128)(2,1)} %copy.26), calls=%async_computation.1 | async-start | bytes 1572864 | tf_op jit(solution)/shard_map/all_to_all | solution.py:29
  32.2 53.9 %all-to-all-start = ((bf16[16,12,4096]{2,1,0:T(8,128)(2,1)}), bf16[16,12,4096]{2,1,0:T(8,128)(2,1)}, u32[]{:S(2)}, u32[]{:S(2)}) async-start(bf16[16,12,4096]{2,1,0:T(8,128)(2,1)} %reshape.40), calls=%async_computation | async-start | bytes 4194304 | tf_op jit(solution)/shard_map/all_to_all | solution.py:63
  86.1 52.8 %all-to-all-start.2 = ((bf16[4,256,1024]{2,1,0:T(8,128)(2,1)}), bf16[4,256,1024]{2,1,0:T(8,128)(2,1)}, u32[]{:S(2)}, u32[]{:S(2)}) async-start(bf16[4,256,1024]{2,1,0:T(8,128)(2,1)} %copy.29), calls=%async_computation.2 | async-start | bytes 4194304 | tf_op jit(solution)/shard_map/all_to_all | solution.py:30
  109.9 33.0 %copy-start.4 = (bf16[1,768,256]{2,1,0:T(8,128)(2,1)S(1)}, bf16[1,768,256]{2,1,0:T(8,128)(2,1)}, u32[]{:S(2)}) copy-start(bf16[1,768,256]{2,1,0:T(8,128)(2,1)} %param.13) | copy-start | bytes 1179652
  152.8 4.6 %copy-start.3 = (bf16[16,8]{0,1:T(8,128)(2,1)S(1)}, bf16[16,8]{0,1:T(8,128)(2,1)}, u32[]{:S(2)}) copy-start(bf16[16,8]{0,1:T(8,128)(2,1)} %param.10) | copy-start | bytes 772
  152.8 54.0 %all-to-all-start.3 = ((bf16[16,12,4096]{2,1,0:T(8,128)(2,1)}), bf16[16,12,4096]{2,1,0:T(8,128)(2,1)}, u32[]{:S(2)}, u32[]{:S(2)}) async-start(bf16[16,12,4096]{2,1,0:T(8,128)(2,1)} %reshape.42), calls=%async_computation.3 | async-start | bytes 4194304 | tf_op jit(solution)/shard_map/all_to_all | solution.py:70
where the time goes:
time: 214 us; the launch traced here: 213 us
  waiting for transfers between devices  128 us (60%)
  matrix products  38.6 us (18%)
  local copies, waits for them, and re-layouts  25.4 us (12%)
  starting transfers between devices  19.9 us (9%)
    all_to_all x1, waiting for transfers between devices, shards(): lax.all_to_all(finished, ('ep', 'col'), split_axis=0, concat_axis=0, tile...  49.2 us
    all_to_all x1, waiting for transfers between devices, shards(): lax.all_to_all(outgoing, ('ep', 'col'), split_axis=0, concat_axis=0, tile...  36 us
    all_to_all x1, waiting for transfers between devices, shards(): lax.all_to_all(span_out, 'col', split_axis=0, concat_axis=2, tiled=True)  29 us
    all_to_all x1, waiting for transfers between devices, shards(): lax.all_to_all(span_in, 'col', split_axis=0, concat_axis=2, tiled=True)  14.2 us
    dot_general x1, matrix products, shards(): jnp.einsum('ej,jrc->erc', mix_coef[:, 1, :], basis_out.astype(jnp.float32...  11.4 us
    dot_general x1, matrix products, shards(): upper = jnp.dot(flat_rows, w_up, preferred_element_type=jnp.float32)  6.6 us
    dot_general x1, matrix products, shards(): gate = jnp.dot(flat_rows, w_gate, preferred_element_type=jnp.float32)  6.58 us
    dot_general x1, matrix products, shards(): jnp.dot(hidden, w_down, preferred_element_type=jnp.float32)  6.56 us
  transfers between devices with their start and end apart: 4, of which 4 were waited for; matrix products, arithmetic and copies ran while one was open for 18% of the time, Pallas kernels for 0%

commit v1 on v0

v1 whole, which is shorter than its diff:
```python
import jax
import jax.numpy as jnp
from jax import lax
from jax.sharding import PartitionSpec as P


def shards(tokens, expert_ids, gate_weights, mix_coef, factor_in, factor_out, basis_in, basis_out):
    tok_count, width = tokens.shape
    hidden_units = factor_out.shape[1]
    bases, rank, col_width = basis_out.shape
    count_ep = lax.axis_size("ep")
    count_col = lax.axis_size("col")
    experts = count_ep * count_col
    me = lax.axis_index("ep") * count_col + lax.axis_index("col")
    group_rows = count_col * tok_count
    onehot = expert_ids[:, :, None] == jnp.arange(experts, dtype=jnp.int32)[None, None, :]
    dense = jnp.sum(
        jnp.where(onehot, gate_weights.astype(jnp.float32)[:, :, None], 0.0), axis=1
    ).astype(jnp.bfloat16)
    dense_all = lax.all_gather(dense, ("ep", "col"), axis=0, tiled=True)
    coef_all = lax.all_gather(mix_coef[:, 1, :], "ep", axis=0, tiled=True)
    rows = lax.all_gather(tokens, ("ep", "col"), axis=0, tiled=True)
    span_in = jnp.einsum(
        "ej,jrc->erc",
        mix_coef[:, 0, :],
        basis_in.astype(jnp.float32),
        precision=lax.Precision.HIGHEST,
    ).astype(jnp.bfloat16)
    mix_in = lax.all_to_all(span_in, "col", split_axis=0, concat_axis=2, tiled=True)[0]
    low_gate = jnp.dot(rows, factor_in[0, 0], preferred_element_type=jnp.float32).astype(
        jnp.bfloat16
    )
    low_up = jnp.dot(rows, factor_in[0, 1], preferred_element_type=jnp.float32).astype(jnp.bfloat16)
    gate = jnp.dot(low_gate, mix_in[:, :hidden_units], preferred_element_type=jnp.float32)
    upper = jnp.dot(low_up, mix_in[:, hidden_units:], preferred_element_type=jnp.float32)
    hidden = (jax.nn.silu(gate) * upper).astype(jnp.bfloat16)
    low_out = jnp.dot(hidden, factor_out[0], preferred_element_type=jnp.float32)
    weight = lax.dynamic_slice_in_dim(dense_all, me, 1, axis=1).astype(jnp.float32)
    low_out = (low_out * weight).astype(jnp.bfloat16)
    low_out = low_out.reshape(count_ep, group_rows, rank)
    swapped = lax.all_to_all(low_out, "ep", split_axis=0, concat_axis=0, tiled=True)
    every = lax.all_gather(swapped, "col", axis=1)
    every = every.reshape(experts, group_rows, rank)
    spread = jnp.einsum("ej,etr->tjr", coef_all, every.astype(jnp.float32), precision=lax.Precision.HIGHEST)
    spread = spread.astype(jnp.bfloat16).reshape(group_rows, bases * rank)
    block = jnp.dot(
        spread, basis_out.reshape(bases * rank, col_width), preferred_element_type=jnp.float32
    ).astype(jnp.bfloat16)
    return lax.all_to_all(block, "col", split_axis=0, concat_axis=1, tiled=True)


def solution(mesh):
    return jax.shard_map(
        shards,
        mesh=mesh,
        in_specs=(
            P(("groups", "ep", "col"), None),
            P(("groups", "ep", "col"), None),
            P(("groups", "ep", "col"), None),
            P("ep", None, None),
            P(("ep", "col"), None, None, None),
            P(("ep", "col"), None, None),
            P(None, None, "col"),
            P(None, None, "col"),
        ),
        out_specs=P(("groups", "ep", "col"), None),
        check_vma=False,
    )
```

time: 214 us -> 127 us (0.59)
  waiting for transfers between devices: 128 us -> 0.72 us
  blocking collectives: 0 us -> 77.9 us
  local copies, waits for them, and re-layouts: 25.4 us -> 5.27 us
  matrix products: 38.6 us -> 18.8 us
  between operations: 0.11 us -> 13.4 us
  starting transfers between devices: 19.9 us -> 9.64 us
    all_to_all x4 -> x2, waiting for transfers between devices: 128 us -> 0.01 us  [the longest x1 0.01 us: shards(): lax.all_to_all(low_out, 'ep', split_axis=0, concat_axis=0, tiled=True)]
    all_gather x0 -> x3, blocking collectives: none -> 69.6 us  [the longest x1 48 us: shards(): dense_all = lax.all_gather(dense, ('ep', 'col'), axis=0, tiled=True)]
    dot_general x6 -> x5, matrix products: 35.8 us -> 16.1 us  [the longest x1 4.99 us: shards(): jnp.dot(spread, basis_out.reshape(bases * rank, col_width), preferred_ele...]
    reshape x5 -> x0, local copies, waits for them, and re-layouts: 14 us -> none  [the longest x1 3.58 us: shards(): returned = returned.reshape(experts * capacity, width)]
    all_to_all x4 -> x2, starting transfers between devices: 19.9 us -> 9.64 us  [the longest x1 6.32 us: shards(): lax.all_to_all(span_in, 'col', split_axis=0, concat_axis=2, tiled=True)[0]]
    all_to_all x0 -> x1, blocking collectives: none -> 8.31 us  [shards(): return lax.all_to_all(block, 'col', split_axis=0, concat_axis=1, tiled=True)]
    all_to_all x2, local copies, waits for them, and re-layouts: 6.32 us -> 2.96 us  [the longest x1 2.3 us: shards(): lax.all_to_all(span_in, 'col', split_axis=0, concat_axis=2, tiled=True)[0]]
  transfers between devices with their start and end apart: 4 -> 3, of which waited for: 4 -> 0; matrix products, arithmetic and copies ran while one was open for 18% -> 6% of each run, Pallas kernels for 0% -> 0%
where the time goes in v1:
time: 127 us; the launch traced here: 126 us
  blocking collectives  77.9 us (61%)
  matrix products  18.8 us (15%)
  between operations  13.4 us (11%)
  starting transfers between devices  9.64 us (8%)
  local copies, waits for them, and re-layouts  5.27 us (4%)
    all_gather x1, blocking collectives, shards(): dense_all = lax.all_gather(dense, ('ep', 'col'), axis=0, tiled=True)  48 us
    all_gather x1, blocking collectives, shards(): every = lax.all_gather(swapped, 'col', axis=1)  16.1 us
    all_to_all x1, blocking collectives, shards(): return lax.all_to_all(block, 'col', split_axis=0, concat_axis=1, tiled=True)  8.31 us
    all_to_all x1, starting transfers between devices, shards(): lax.all_to_all(span_in, 'col', split_axis=0, concat_axis=2, tiled=True)[0]  6.32 us
    all_gather x1, blocking collectives, shards(): coef_all = lax.all_gather(mix_coef[:, 1, :], 'ep', axis=0, tiled=True)  5.54 us
    dot_general x1, matrix products, shards(): jnp.dot(spread, basis_out.reshape(bases * rank, col_width), preferred_ele...  4.99 us
    dot_general x1, matrix products, shards(): jnp.dot(low_gate, mix_in[:, :hidden_units], preferred_element_type=jnp.fl...  4.3 us
    dot_general x1, matrix products, shards(): jnp.dot(rows, factor_in[0, 1], preferred_element_type=jnp.float32)  3.59 us
  transfers between devices with their start and end apart: 3, of which 0 were waited for; matrix products, arithmetic and copies ran while one was open for 6% of the time, Pallas kernels for 0%

profile of v1, /device:TPU:0, one launch (start us, length us, event | category | flops | bytes accessed | tf_op | source)
XLA Modules:
  0.0 126.1 jit_solution(1152123499494605069)
XLA Ops:
  6.5 0.7 all-gather.4.cloned.1.call-update
  7.3 0.9 fusion.39
  8.2 0.2 copy-done
  8.4 2.8 %fusion.8 = bf16[4,256,384]{2,0,1:T(4,128)(2,1)S(1)} fusion(f32[4,16,1]{1,0,2:T(4,128)S(1)} %bitcast.49, bf16[16,256,384]{2,1,0:T(8,128)(2,1)S(1)} %copy-done), kind=kOutput, calls=%fused_computation.8 | convolution fusion | flops 75890688 | bytes 3932416 | tf_op jit(solution)/shard_map/ej,jrc->erc/dot_general | solution.py:23
  11.2 1.0 copy.34
  12.2 6.3 %all-to-all-start = ((bf16[4,256,384]{2,1,0:T(8,128)(2,1)}), bf16[4,256,384]{2,1,0:T(8,128)(2,1)}, u32[]{:S(2)}, u32[]{:S(2)}) async-start(bf16[4,256,384]{2,1,0:T(8,128)(2,1)} %copy.34), calls=%async_computation | async-start | bytes 1572864 | tf_op jit(solution)/shard_map/all_to_all | solution.py:29
  18.5 0.1 copy.36
  18.6 0.1 copy.37
  18.7 0.1 select_reduce_fusion
  18.8 48.0 %all_gather.16 = bf16[256,16]{1,0:T(8,128)(2,1)S(1)} all-gather(bf16[16,16]{1,0:T(8,128)(2,1)S(1)} %select_reduce_fusion), channel_id=1, replica_groups=mesh['groups'=2,'ep'=4,'col'=4] {'ep','col'}, dimensions={0}, use_global_device_ids=true | all-gather | bytes 8704 | tf_op jit(solution)/shard_map/all_gather | solution.py:20
  66.8 0.2 convert_reduce_fusion
  66.9 0.0 all-to-all-done
  66.9 2.3 %copy.35 = bf16[4,256,384]{1,2,0:T(8,128)(2,1)} copy(bf16[4,256,384]{2,1,0:T(8,128)(2,1)} %all-to-all-done) | data formatting | bytes 1572864 | tf_op jit(solution)/shard_map/all_to_all | solution.py:29
  69.2 3.6 %fusion.20 = bf16[256,256]{1,0:T(8,128)(2,1)} fusion(bf16[256,4096]{1,0:T(8,128)(2,1)} %all-gather.4.cloned.1.call-done, bf16[1,2,4096,256]{3,2,1,0:T(8,128)(2,1)} %param.12), kind=kOutput, calls=%fused_computation.19 | convolution fusion | flops 536936448 | bytes 4325376 | tf_op jit(solution)/shard_map/dot_general | solution.py:33
  72.8 4.3 %fusion.24 = f32[256,768]{1,0:T(8,128)} fusion(bf16[256,4096]{1,0:T(8,128)(2,1)} %all-gather.4.cloned.1.call-done, bf16[1,2,4096,256]{3,2,1,0:T(8,128)(2,1)} %param.12, bf16[256,1536]{0,1:T(8,128)(2,1)} %bitcast.44), kind=kOutput, calls=%fused_computation.20 | convolution fusion | flops 637599744 | bytes 5373952 | tf_op jit(solution)/shard_map/dot_general | solution.py:34
  77.1 2.5 %fusion.16 = bf16[256,256]{1,0:T(8,128)(2,1)} fusion(bf16[256,256]{1,0:T(8,128)(2,1)} %fusion.20, f32[256,768]{1,0:T(8,128)} %fusion.24, bf16[256,1536]{0,1:T(8,128)(2,1)} %bitcast.45, bf16[1,768,256]{2,1,0:T(8,128)(2,1)S(1)} %copy-done.3, f32[256]{0:T(256)S(1)} %convert_reduce_fusion), kind=kOutput, calls=%fused_computation.17 | convolution fusion | flops 202637312 | bytes 1836032 | tf_op jit(solution)/shard_map/dot_general | solution.py:37
  79.6 3.3 %all-to-all-start.1 = ((bf16[4,64,256]{2,1,0:T(8,128)(2,1)}), bf16[4,64,256]{2,1,0:T(8,128)(2,1)S(1)}, u32[]{:S(2)}, u32[]{:S(2)}) async-start(bf16[4,64,256]{2,1,0:T(8,128)(2,1)} %bitcast.10), calls=%async_computation.1 | async-start | bytes 262144 | tf_op jit(solution)/shard_map/all_to_all | solution.py:41
  82.9 5.5 %all-gather.1 = f32[16,1,16]{2,1,0:T(1,128)S(1)} all-gather(f32[4,1,16]{2,1,0:T(1,128)S(1)} %get-tuple-element.6), channel_id=3, replica_groups=mesh['groups'=2,'ep'=4,'col'=4] {'ep'}, dimensions={0}, use_global_device_ids=true | all-gather | bytes 1280 | tf_op jit(solution)/shard_map/all_gather | solution.py:21
  88.5 0.0 all-to-all-done.1
  88.5 16.1 %all-gather = bf16[4,256,256]{2,1,0:T(8,128)(2,1)S(1)} all-gather(bf16[4,64,256]{2,1,0:T(8,128)(2,1)S(1)} %all-to-all-done.1), channel_id=2, replica_groups=mesh['groups'=2,'ep'=4,'col'=4] {'col'}, dimensions={1}, use_global_device_ids=true | all-gather | bytes 655360 | tf_op jit(solution)/shard_map/all_gather | solution.py:42
  104.6 0.7 fusion.12
  105.3 5.0 %fusion.15 = bf16[64,1024]{1,0:T(8,128)(2,1)S(1)} fusion(bf16[16,256,1024]{2,1,0:T(8,128)(2,1)} %param.15, bf16[64,16,256]{2,1,0:T(8,128)(2,1)S(1)} %fusion.12), kind=kOutput, calls=%fused_computation.16 | convolution fusion | flops 536936448 | bytes 9043968 | tf_op jit(solution)/shard_map/dot_general | solution.py:46
  110.3 8.3 %all_to_all.39 = bf16[4,16,1024]{2,1,0:T(8,128)(2,1)S(1)} all-to-all(bf16[4,16,1024]{2,1,0:T(8,128)(2,1)S(1)} %bitcast.46), channel_id=1, replica_groups=mesh['groups'=2,'ep'=4,'col'=4] {'col'}, dimensions={0} | all-to-all | bytes 262144 | tf_op jit(solution)/shard_map/all_to_all | solution.py:49
  118.6 0.7 copy.42
  (9 shorter events, 0.0 us)
Async XLA Ops:
  6.5 1.9 %copy-start = (bf16[16,256,384]{2,1,0:T(8,128)(2,1)S(1)}, bf16[16,256,384]{2,1,0:T(8,128)(2,1)}, u32[]{:S(2)}) copy-start(bf16[16,256,384]{2,1,0:T(8,128)(2,1)} %param.14) | copy-start | bytes 9437188
  6.5 62.7 %all-gather.4.cloned.1.call-start = ((), (), s32[]{:S(2)}) async-start(), calls=%async_computation.3 | async-start | bytes 2228224 | tf_op jit(solution)/shard_map/all_gather | solution.py:22
  8.4 10.1 %copy-start.1 = (s32[16,8]{0,1:T(8,128)S(1)}, s32[16,8]{0,1:T(8,128)}, u32[]{:S(2)}) copy-start(s32[16,8]{0,1:T(8,128)} %param.9) | copy-start | bytes 1540
  8.4 10.1 %copy-start.2 = (bf16[16,8]{0,1:T(8,128)(2,1)S(1)}, bf16[16,8]{0,1:T(8,128)(2,1)}, u32[]{:S(2)}) copy-start(bf16[16,8]{0,1:T(8,128)(2,1)} %param.10) | copy-start | bytes 772
  12.2 54.8 %all-to-all-start = ((bf16[4,256,384]{2,1,0:T(8,128)(2,1)}), bf16[4,256,384]{2,1,0:T(8,128)(2,1)}, u32[]{:S(2)}, u32[]{:S(2)}) async-start(bf16[4,256,384]{2,1,0:T(8,128)(2,1)} %copy.34), calls=%async_computation | async-start | bytes 1572864 | tf_op jit(solution)/shard_map/all_to_all | solution.py:29
  72.8 4.3 %copy-start.3 = (bf16[1,768,256]{2,1,0:T(8,128)(2,1)S(1)}, bf16[1,768,256]{2,1,0:T(8,128)(2,1)}, u32[]{:S(2)}) copy-start(bf16[1,768,256]{2,1,0:T(8,128)(2,1)} %param.13) | copy-start | bytes 1179652
  79.6 8.9 %all-to-all-start.1 = ((bf16[4,64,256]{2,1,0:T(8,128)(2,1)}), bf16[4,64,256]{2,1,0:T(8,128)(2,1)S(1)}, u32[]{:S(2)}, u32[]{:S(2)}) async-start(bf16[4,64,256]{2,1,0:T(8,128)(2,1)} %bitcast.10), calls=%async_computation.1 | async-start | bytes 262144 | tf_op jit(solution)/shard_map/all_to_all | solution.py:41
Sparse Core Ops, SparseCore 0:
  9.6 51.2 all-gather.3

commit v2 on v1

--- a/solution.py
+++ b/solution.py
@@ -1,7 +1,343 @@
+import functools
+
 import jax
 import jax.numpy as jnp
 from jax import lax
+from jax.experimental import pallas as pl
+from jax.experimental.pallas import tpu as pltpu
 from jax.sharding import PartitionSpec as P
+
+F32, BF16 = jnp.float32, jnp.bfloat16
+
+
+def dot(a, b):
+    return jnp.dot(a, b, preferred_element_type=F32)
+
+
+def fused(
+    E, C, ids_ref, gates_ref, coef_smem, coef_vmem, tok_ref, fin_hbm, fout_hbm, bin_hbm, bout_hbm,
+    out_ref,
+    xall, fin, fout, bin_, bout, mstage, mix, call, call_s, low, zstage, zall, spread, ostage, oall,
+    load_sem, coef_s_sem, s_left, s_right, s_y, s_sib, x_recv, m_send, m_recv, g_send, g_recv,
+    c_send, c_recv, z_send, z_recv, o_send, o_recv,
+):
+    g, i, c = lax.axis_index("groups"), lax.axis_index("ep"), lax.axis_index("col")
+    T, D = tok_ref.shape
+    H, W = mix.shape[2], mix.shape[3]
+    OW = oall.shape[2]
+    R = low.shape[3]
+    J = bin_.shape[0]
+    hidden_units = fout.shape[0]
+    i_y = (i + 2) % E
+    i_s = (i // 2) * 2 + (i + 1) % 2
+    i_d = (i_s + 2) % E
+    me = i * C + c
+
+    def remote(src, dst, ss, rs, dev):
+        return pltpu.make_async_remote_copy(
+            src_ref=src, dst_ref=dst, send_sem=ss, recv_sem=rs, device_id=dev,
+            device_id_type=pl.DeviceIdType.MESH,
+        )
+
+    loads = [
+        pltpu.make_async_copy(bin_hbm.at[:, pl.ds(pl.multiple_of(g * H, H), H), :], bin_, load_sem.at[0]),
+        pltpu.make_async_copy(fin_hbm.at[0], fin, load_sem.at[1]),
+        pltpu.make_async_copy(fout_hbm.at[0], fout, load_sem.at[2]),
+        pltpu.make_async_copy(bout_hbm, bout, load_sem.at[3]),
+    ]
+    for ld in loads:
+        ld.start()
+
+    barrier = pltpu.get_barrier_semaphore()
+    for k in range(1, E * C):
+        o = (me + k) % (E * C)
+        pl.semaphore_signal(barrier, inc=1, device_id=(g, o // C, o % C), device_id_type=pl.DeviceIdType.MESH)
+    pl.semaphore_signal(barrier, inc=1, device_id=(1 - g, i, c), device_id_type=pl.DeviceIdType.MESH)
+
+    xall[i, c, :, :D] = tok_ref[...]
+    lane = lax.broadcasted_iota(jnp.int32, (T, 128), 1)
+    table = jnp.zeros((T, 128), F32)
+    for k in range(ids_ref.shape[1]):
+        table += jnp.where(lane == ids_ref[:, k : k + 1], gates_ref[:, k : k + 1].astype(F32), 0.0)
+    xall[i, c, :, D:] = table.astype(BF16)
+    call[i] = jnp.zeros((8, 128), F32)
+    call[i, :C, :J] = coef_vmem[:, 1, :]
+    pl.semaphore_wait(barrier, E * C)
+
+    def right(line_c):
+        blk = xall.at[i, line_c]
+        return remote(blk, blk, s_right.at[line_c], x_recv.at[i, line_c], (g, i, c + 1))
+
+    def left(line_c):
+        blk = xall.at[i, line_c]
+        return remote(blk, blk, s_left.at[line_c], x_recv.at[i, line_c], (g, i, c - 1))
+
+    def over(line_c):
+        blk = xall.at[i, line_c]
+        return remote(blk, blk, s_y.at[line_c], x_recv.at[i, line_c], (g, i_y, c))
+
+    def sib(which, line_c):
+        line = i if which == 0 else i_y
+        blk = xall.at[line, line_c]
+        return remote(blk, blk, s_sib.at[which, line_c], x_recv.at[line, line_c], (g, i_s, c))
+
+    def arrive(line, line_c):
+        blk = xall.at[line, line_c]
+        remote(blk, blk, s_y.at[0], x_recv.at[line, line_c], (g, i_y, c)).wait_recv()
+
+    @pl.when(c < C - 1)
+    def _():
+        right(c).start()
+
+    @pl.when(c > 0)
+    def _():
+        left(c).start()
+
+    over(c).start()
+    sib(0, c).start()
+    coefs = []
+    for k in range(1, E):
+        o = (i + k) % E
+        cp = remote(call.at[i], call.at[i], c_send.at[k], c_recv.at[i], (g, o, c))
+        cp.start()
+        coefs.append(cp)
+
+    loads[0].wait()
+    CH = 16
+
+    def mixing(step, carry):
+        rows = pl.ds(pl.multiple_of(step * CH, CH), CH)
+        acc = [None] * C
+        for j in range(J):
+            b = bin_[j, rows, :].astype(F32)
+            for e in range(C):
+                v = coef_smem[e, 0, j] * b
+                acc[e] = v if acc[e] is None else acc[e] + v
+        for e in range(C):
+            mstage[e, rows, :] = acc[e].astype(BF16)
+        return carry
+
+    lax.fori_loop(0, H // CH, mixing, 0)
+
+    def mix_to(dest):
+        return remote(mstage.at[dest], mix.at[g, c], m_send.at[dest], m_recv.at[c], (g, i, dest))
+
+    def mix_from(src):
+        return remote(mstage.at[c], mix.at[g, src], m_send.at[c], m_recv.at[src], (g, i, src))
+
+    def mix_cross(src):
+        return remote(mix.at[g, src], mix.at[g, src], g_send.at[src], g_recv.at[src], (1 - g, i, c))
+
+    for d in range(C - 1, 0, -1):
+        @pl.when(c - d >= 0)
+        def _():
+            mix_to(c - d).start()
+
+        @pl.when(c + d < C)
+        def _():
+            mix_to(c + d).start()
+
+    mix[g, c] = mstage[c]
+    mix_cross(c).start()
+
+    def arrive_b(d):
+        for s in ((0,) if d == 0 else (-d, d)):
+            src = c + s
+
+            @pl.when((src >= 0) & (src < C))
+            def _():
+                arrive(i_y, src)
+                sib(1, src).start()
+
+    for d in range(1, C):
+        @pl.when(c - d >= 0)
+        def _():
+            arrive(i, c - d)
+
+            @pl.when(c < C - 1)
+            def _():
+                right(c - d).start()
+
+            over(c - d).start()
+            sib(0, c - d).start()
+
+        @pl.when(c + d < C)
+        def _():
+            arrive(i, c + d)
+
+            @pl.when(c > 0)
+            def _():
+                left(c + d).start()
+
+            over(c + d).start()
+            sib(0, c + d).start()
+
+        arrive_b(d - 1)
+        for s in (-d, d):
+            src = c + s
+
+            @pl.when((src >= 0) & (src < C))
+            def _():
+                mix_from(src).wait_recv()
+                mix_cross(src).start()
+
+    loads[1].wait()
+
+    def project(line):
+        rows = xall[line].reshape(C * T, D + 128)[:, :D]
+        low[line, 0] = dot(rows, fin[0]).astype(BF16)
+        low[line, 1] = dot(rows, fin[1]).astype(BF16)
+
+    project(i)
+    arrive_b(C - 1)
+    for k in range(C):
+        arrive(i_s, k)
+    for k in range(C):
+        arrive(i_d, k)
+    lax.fori_loop(1, E, lambda k, carry: (project((i + k) % E), carry)[1], 0)
+    for k in range(C):
+        remote(mix.at[g, k], mix.at[1 - g, k], g_send.at[k], g_recv.at[k], (1 - g, i, c)).wait_recv()
+    loads[2].wait()
+
+    wide = lax.broadcasted_iota(jnp.int32, (C * T, 128), 1)
+
+    def expert(k, carry):
+        line = (i + k) % E
+        parts = []
+        for b in range(C // 2):
+            mg = jnp.concatenate([mix[0, b], mix[1, b]], axis=0)
+            mu = jnp.concatenate([mix[0, C // 2 + b], mix[1, C // 2 + b]], axis=0)
+            gate = dot(low[line, 0], mg)
+            upper = dot(low[line, 1], mu)
+            parts.append((gate / (1.0 + jnp.exp(-gate)) * upper).astype(BF16))
+        hidden = jnp.concatenate(parts, axis=1)
+        z = dot(hidden, fout[...])
+        table = xall[line].reshape(C * T, D + 128)[:, D:].astype(F32)
+        weight = jnp.sum(jnp.where(wide == me, table, 0.0), axis=1, keepdims=True)
+        zstage[line] = (z * weight).astype(BF16)
+        return carry
+
+    def z_to(line, dest):
+        return remote(zstage.at[line], zall.at[me], z_send.at[line, dest], z_recv.at[me], (g, line, dest))
+
+    for k in list(range(1, E)) + [0]:
+        line = (i + k) % E
+        expert(k, 0)
+        for m in range(C):
+            dest = (c + m) % C
+            if k or m:
+                z_to(line, dest).start()
+    zall[me] = zstage[i]
+
+    for k in range(1, E):
+        o = (i + k) % E
+        remote(call.at[o], call.at[o], c_send.at[k], c_recv.at[o], (g, o, c)).wait_recv()
+    cc = pltpu.make_async_copy(call, call_s, coef_s_sem)
+    cc.start()
+    cc.wait()
+    loads[3].wait()
+    for k in range(1, E * C):
+        o = (me + k) % (E * C)
+        remote(zstage.at[i], zall.at[o], z_send.at[i, c], z_recv.at[o], (g, o // C, o % C)).wait_recv()
+
+    for col in range(R // 128):
+        lanes = slice(col * 128, (col + 1) * 128)
+
+        def combine(step, carry):
+            rows = pl.ds(pl.multiple_of(step * 16, 16), 16)
+            z = [zall[e, rows, lanes].astype(F32) for e in range(E * C)]
+            for j in range(J):
+                acc = call_s[0, 0, j] * z[0]
+                for e in range(1, E * C):
+                    acc = acc + call_s[e // C, e % C, j] * z[e]
+                spread[rows, j * R + col * 128 : j * R + (col + 1) * 128] = acc.astype(BF16)
+            return carry
+
+        lax.fori_loop(0, C * T // 16, combine, 0)
+
+    step_w = 256
+    for n in range(OW // step_w):
+        cols = slice(n * step_w, (n + 1) * step_w)
+        block = dot(spread[...], bout[:, cols]).astype(BF16)
+        ostage[:, :, cols] = block.reshape(C, T, step_w)
+
+    def o_to(dest):
+        return remote(ostage.at[dest], oall.at[c], o_send.at[dest], o_recv.at[c], (g, i, dest))
+
+    for k in range(1, C):
+        o_to((c + k) % C).start()
+    oall[c] = ostage[c]
+    for k in range(1, C):
+        o = (c + k) % C
+        remote(ostage.at[o], oall.at[o], o_send.at[o], o_recv.at[o], (g, i, o)).wait_recv()
+    for k in range(C):
+        out_ref[:, k * OW : (k + 1) * OW] = oall[k]
+
+    for k in range(C):
+        @pl.when((c < C - 1) & (k <= c))
+        def _():
+            right(k).wait_send()
+
+        @pl.when((c > 0) & (k >= c))
+        def _():
+            left(k).wait_send()
+
+        over(k).wait_send()
+        sib(0, k).wait_send()
+        sib(1, k).wait_send()
+        mix_cross(k).wait_send()
+    for cp in coefs:
+        cp.wait_send()
+    for k in range(1, C):
+        mix_to((c + k) % C).wait_send()
+        o_to((c + k) % C).wait_send()
+    for k in range(E):
+        for m in range(C):
+            if k or m:
+                z_to((i + k) % E, (c + m) % C).wait_send()
+
+
+def shards_kernel(E, C, tokens, expert_ids, gate_weights, mix_coef, factor_in, factor_out, basis_in, basis_out):
+    T, D = tokens.shape
+    J, R, W = basis_in.shape
+    OW = basis_out.shape[2]
+    FFU = factor_out.shape[1]
+    H = R // 2
+    vm = pl.BlockSpec(memory_space=pltpu.VMEM)
+    anym = pl.BlockSpec(memory_space=pl.ANY)
+    dma = pltpu.SemaphoreType.DMA
+    return pl.pallas_call(
+        functools.partial(fused, E, C),
+        out_shape=jax.ShapeDtypeStruct((T, D), BF16),
+        in_specs=[vm, vm, pl.BlockSpec(memory_space=pltpu.SMEM), vm, vm, anym, anym, anym, anym],
+        out_specs=vm,
+        scratch_shapes=[
+            pltpu.VMEM((E, C, T, D + 128), BF16),
+            pltpu.VMEM((2, D, R), BF16),
+            pltpu.VMEM((FFU, R), BF16),
+            pltpu.VMEM((J, H, W), BF16),
+            pltpu.VMEM((J * R, OW), BF16),
+            pltpu.VMEM((C, H, W), BF16),
+            pltpu.VMEM((2, C, H, W), BF16),
+            pltpu.VMEM((E, 8, 128), F32),
+            pltpu.SMEM((E, 8, 128), F32),
+            pltpu.VMEM((E, 2, C * T, R), BF16),
+            pltpu.VMEM((E, C * T, R), BF16),
+            pltpu.VMEM((E * C, C * T, R), BF16),
+            pltpu.VMEM((C * T, J * R), BF16),
+            pltpu.VMEM((C, T, OW), BF16),
+            pltpu.VMEM((C, T, OW), BF16),
+            dma((4,)), dma, dma((C,)), dma((C,)), dma((C,)), dma((2, C)), dma((E, C)),
+            dma((C,)), dma((C,)), dma((C,)), dma((C,)),
+            dma((E,)), dma((E,)), dma((E, C)), dma((E * C,)), dma((C,)), dma((C,)),
+        ],
+        compiler_params=pltpu.CompilerParams(
+            collective_id=0, has_side_effects=True, vmem_limit_bytes=48 * 1024 * 1024
+        ),
+    )(
+        expert_ids, gate_weights, mix_coef, mix_coef, tokens, factor_in, factor_out, basis_in,
+        basis_out.reshape(J * R, OW),
+    )
 
 
 def shards(tokens, expert_ids, gate_weights, mix_coef, factor_in, factor_out, basis_in, basis_out):
@@ -50,8 +386,10 @@
 
 
 def solution(mesh):
+    E, C = mesh.shape["ep"], mesh.shape["col"]
+    small = E == 4 and C == 4 and mesh.shape["groups"] == 2
     return jax.shard_map(
-        shards,
+        functools.partial(shards_kernel, E, C) if small else shards,
         mesh=mesh,
         in_specs=(
             P(("groups", "ep", "col"), None),

time: 127 us -> 59.7 us (0.47)
  blocking collectives: 77.9 us -> 0 us
  Pallas kernels: 0 us -> 52.7 us
  matrix products: 18.8 us -> 0 us
  between operations: 13.4 us -> 0.01 us
  starting transfers between devices: 9.64 us -> 0 us
  local copies, waits for them, and re-layouts: 5.27 us -> 6.65 us
    all_gather x3 -> x0, blocking collectives: 69.6 us -> none  [the longest x1 48 us: shards(): dense_all = lax.all_gather(dense, ('ep', 'col'), axis=0, tiled=True)]
    pallas_call x0 -> x1, Pallas kernels: none -> 52.7 us  [shards_kernel(): pl.pallas_call(functools.partial(fused, E, C), out_shape=jax.ShapeDtypeSt...]
    dot_general x6 -> x0, matrix products: 18.8 us -> none  [the longest x1 4.99 us: shards(): jnp.dot(spread, basis_out.reshape(bases * rank, col_width), preferred_ele...]
    all_to_all x2 -> x0, starting transfers between devices: 9.64 us -> none  [the longest x1 6.32 us: shards(): lax.all_to_all(span_in, 'col', split_axis=0, concat_axis=2, tiled=True)[0]]
    all_to_all x1 -> x0, blocking collectives: 8.31 us -> none  [shards(): return lax.all_to_all(block, 'col', split_axis=0, concat_axis=1, tiled=True)]
    unnamed x9 -> x11, local copies, waits for them, and re-layouts: 0.32 us -> 6.65 us
    all_to_all x2 -> x0, local copies, waits for them, and re-layouts: 2.96 us -> none  [the longest x1 2.3 us: shards(): lax.all_to_all(span_in, 'col', split_axis=0, concat_axis=2, tiled=True)[0]]
  transfers between devices with their start and end apart: 3 -> 0, of which waited for: 0 -> 0; matrix products, arithmetic and copies ran while one was open for 6% -> 0% of each run, Pallas kernels for 0% -> 0%
where the time goes in v2:
time: 59.7 us; the launch traced here: 59.4 us
  Pallas kernels  52.7 us (88%)
  local copies, waits for them, and re-layouts  6.65 us (11%)
    pallas_call x1, Pallas kernels, shards_kernel(): pl.pallas_call(functools.partial(fused, E, C), out_shape=jax.ShapeDtypeSt...  52.7 us
    unnamed x11, local copies, waits for them, and re-layouts  6.65 us

profile of v2, /device:TPU:0, one launch (start us, length us, event | category | flops | bytes accessed | tf_op | source)
XLA Modules:
  0.0 59.4 jit_solution(2285997904998886169)
XLA Ops:
  0.0 0.8 %copy.10.gates_ref = bf16[16,8]{1,0:T(8,128)(2,1)S(1)} copy(bf16[16,8]{0,1:T(8,128)(2,1)} %param.10) | data formatting | bytes 512 | tf_op args[2]
  0.8 0.8 %copy.9.ids_ref = s32[16,8]{1,0:T(8,128)S(1)} copy(s32[16,8]{0,1:T(8,128)} %param.9) | data formatting | bytes 1024 | tf_op args[1]
  1.5 0.0 copy-start
  1.5 1.9 %copy-done = bf16[16,256,384]{2,1,0:T(8,128)(2,1)S(1)} copy-done((bf16[16,256,384]{2,1,0:T(8,128)(2,1)S(1)}, bf16[16,256,384]{2,1,0:T(8,128)(2,1)}, u32[]{:S(2)}) %copy-start) | copy-done | bytes 3145752
  3.4 0.0 copy-start.1
  3.4 1.0 %copy-done.1 = bf16[1,768,256]{2,1,0:T(8,128)(2,1)S(1)} copy-done((bf16[1,768,256]{2,1,0:T(8,128)(2,1)S(1)}, bf16[1,768,256]{2,1,0:T(8,128)(2,1)}, u32[]{:S(2)}) %copy-start.1) | copy-done | bytes 393240
  4.4 0.0 copy-start.2
  4.4 0.9 %copy-done.2 = bf16[16,4096]{1,0:T(8,128)(2,1)S(1)} copy-done((bf16[16,4096]{1,0:T(8,128)(2,1)S(1)}, bf16[16,4096]{1,0:T(8,128)(2,1)}, u32[]{:S(2)}) %copy-start.2) | copy-done | bytes 131096
  5.3 0.0 copy-start.3
  5.3 0.7 %copy-done.3 = f32[4,2,16]{2,1,0:T(2,128)S(1)} copy-done((f32[4,2,16]{2,1,0:T(2,128)S(1)}, f32[4,2,16]{2,1,0:T(2,128)}, u32[]{:S(2)}) %copy-start.3) | copy-done | bytes 536
  6.0 52.7 %shard_map.82 = bf16[16,4096]{1,0:T(8,128)(2,1)S(1)} custom-call(s32[16,8]{1,0:T(8,128)S(1)} %copy.9.ids_ref, bf16[16,8]{1,0:T(8,128)(2,1)S(1)} %copy.10.gates_ref, f32[4,2,16]{2,1,0:T(2,128)S(1)} %copy-done.3, f32[4,2,16]{2,1,0:T(2,128)S(1)} %copy-done.3, bf16[16,4096]{1,0:T(8,128)(2,1)S(1)} %copy-done.2, bf16[1,2,4096,256]{3,2,1,0:T(8,128)(2,1)} %fin_hbm.1, ...), custom_call_target="tpu_custom_call" | custom-call | tf_op jit(solution)/shard_map/pallas_call | solution.py:309
  58.7 0.7 %copy.12 = bf16[16,4096]{1,0:T(8,128)(2,1)} copy(bf16[16,4096]{1,0:T(8,128)(2,1)S(1)} %shard_map.82) | data formatting | bytes 262144
Async XLA Ops:
  1.5 1.9 %copy-start = (bf16[16,256,384]{2,1,0:T(8,128)(2,1)S(1)}, bf16[16,256,384]{2,1,0:T(8,128)(2,1)}, u32[]{:S(2)}) copy-start(bf16[16,256,384]{2,1,0:T(8,128)(2,1)} %bin_hbm.1) | copy-start | bytes 9437188
  3.4 1.0 %copy-start.1 = (bf16[1,768,256]{2,1,0:T(8,128)(2,1)S(1)}, bf16[1,768,256]{2,1,0:T(8,128)(2,1)}, u32[]{:S(2)}) copy-start(bf16[1,768,256]{2,1,0:T(8,128)(2,1)} %fout_hbm.1) | copy-start | bytes 1179652
  4.4 0.9 %copy-start.2 = (bf16[16,4096]{1,0:T(8,128)(2,1)S(1)}, bf16[16,4096]{1,0:T(8,128)(2,1)}, u32[]{:S(2)}) copy-start(bf16[16,4096]{1,0:T(8,128)(2,1)} %tok_ref.1) | copy-start | bytes 393220
  5.3 0.7 %copy-start.3 = (f32[4,2,16]{2,1,0:T(2,128)S(1)}, f32[4,2,16]{2,1,0:T(2,128)}, u32[]{:S(2)}) copy-start(f32[4,2,16]{2,1,0:T(2,128)} %coef_vmem.1) | copy-start | bytes 1540

commit v3 on v2

--- a/solution.py
+++ b/solution.py
@@ -15,16 +15,16 @@
 
 
 def fused(
-    E, C, ids_ref, gates_ref, coef_smem, coef_vmem, tok_ref, fin_hbm, fout_hbm, bin_hbm, bout_hbm,
+    E, C, ids_hbm, gates_hbm, coef_hbm, tok_hbm, fin_hbm, fout_hbm, bin_hbm, bout_hbm,
     out_ref,
-    xall, fin, fout, bin_, bout, mstage, mix, call, call_s, low, zstage, zall, spread, ostage, oall,
-    load_sem, coef_s_sem, s_left, s_right, s_y, s_sib, x_recv, m_send, m_recv, g_send, g_recv,
+    ids_ref, gates_ref, coef_smem, coef_vmem, xall, fin, fout, bin_, bout, mstage, mix, call, call_s, low, zstage, zall, spread, ostage, oall,
+    small_sem, load_sem, coef_s_sem, s_left, s_right, s_y, s_sib, x_recv, m_send, m_recv, g_send, g_recv,
     c_send, c_recv, z_send, z_recv, o_send, o_recv,
 ):
     g, i, c = lax.axis_index("groups"), lax.axis_index("ep"), lax.axis_index("col")
-    T, D = tok_ref.shape
+    T, D = tok_hbm.shape
     H, W = mix.shape[2], mix.shape[3]
-    OW = oall.shape[2]
+    OW = bout.shape[1]
     R = low.shape[3]
     J = bin_.shape[0]
     hidden_units = fout.shape[0]
@@ -39,14 +39,22 @@
             device_id_type=pl.DeviceIdType.MESH,
         )
 
+    small = [
+        pltpu.make_async_copy(ids_hbm, ids_ref, small_sem.at[0]),
+        pltpu.make_async_copy(gates_hbm, gates_ref, small_sem.at[1]),
+        pltpu.make_async_copy(coef_hbm, coef_vmem, small_sem.at[2]),
+        pltpu.make_async_copy(coef_hbm, coef_smem, small_sem.at[3]),
+        pltpu.make_async_copy(tok_hbm, xall.at[i, c, :, pl.ds(0, D)], small_sem.at[4]),
+    ]
+    for ld in small:
+        ld.start()
     loads = [
         pltpu.make_async_copy(bin_hbm.at[:, pl.ds(pl.multiple_of(g * H, H), H), :], bin_, load_sem.at[0]),
         pltpu.make_async_copy(fin_hbm.at[0], fin, load_sem.at[1]),
         pltpu.make_async_copy(fout_hbm.at[0], fout, load_sem.at[2]),
         pltpu.make_async_copy(bout_hbm, bout, load_sem.at[3]),
     ]
-    for ld in loads:
-        ld.start()
+    loads[0].start()
 
     barrier = pltpu.get_barrier_semaphore()
     for k in range(1, E * C):
@@ -54,47 +62,54 @@
         pl.semaphore_signal(barrier, inc=1, device_id=(g, o // C, o % C), device_id_type=pl.DeviceIdType.MESH)
     pl.semaphore_signal(barrier, inc=1, device_id=(1 - g, i, c), device_id_type=pl.DeviceIdType.MESH)
 
-    xall[i, c, :, :D] = tok_ref[...]
-    lane = lax.broadcasted_iota(jnp.int32, (T, 128), 1)
-    table = jnp.zeros((T, 128), F32)
-    for k in range(ids_ref.shape[1]):
-        table += jnp.where(lane == ids_ref[:, k : k + 1], gates_ref[:, k : k + 1].astype(F32), 0.0)
-    xall[i, c, :, D:] = table.astype(BF16)
+    for ld in small:
+        ld.wait()
+    number = lax.broadcasted_iota(jnp.int32, (128, T), 0)
+    table = jnp.zeros((128, T), F32)
+    for k in range(ids_ref.shape[0]):
+        table += jnp.where(number == ids_ref[k : k + 1, :], gates_ref[k : k + 1, :].astype(F32), 0.0)
+    xall[i, c, :, D:] = table.T.astype(BF16)
     call[i] = jnp.zeros((8, 128), F32)
     call[i, :C, :J] = coef_vmem[:, 1, :]
     pl.semaphore_wait(barrier, E * C)
 
-    def right(line_c):
-        blk = xall.at[i, line_c]
-        return remote(blk, blk, s_right.at[line_c], x_recv.at[i, line_c], (g, i, c + 1))
-
-    def left(line_c):
-        blk = xall.at[i, line_c]
-        return remote(blk, blk, s_left.at[line_c], x_recv.at[i, line_c], (g, i, c - 1))
-
-    def over(line_c):
-        blk = xall.at[i, line_c]
-        return remote(blk, blk, s_y.at[line_c], x_recv.at[i, line_c], (g, i_y, c))
-
-    def sib(which, line_c):
+    parts_x = ((0, D // 2), (D // 2, D // 2 + 128))
+
+    def piece(line, line_c, p):
+        return xall.at[line, line_c, :, pl.ds(*parts_x[p])]
+
+    def right(line_c, p):
+        blk = piece(i, line_c, p)
+        return remote(blk, blk, s_right.at[line_c, p], x_recv.at[i, line_c, p], (g, i, c + 1))
+
+    def left(line_c, p):
+        blk = piece(i, line_c, p)
+        return remote(blk, blk, s_left.at[line_c, p], x_recv.at[i, line_c, p], (g, i, c - 1))
+
+    def over(line_c, p):
+        blk = piece(i, line_c, p)
+        return remote(blk, blk, s_y.at[line_c, p], x_recv.at[i, line_c, p], (g, i_y, c))
+
+    def sib(which, line_c, p):
         line = i if which == 0 else i_y
-        blk = xall.at[line, line_c]
-        return remote(blk, blk, s_sib.at[which, line_c], x_recv.at[line, line_c], (g, i_s, c))
-
-    def arrive(line, line_c):
-        blk = xall.at[line, line_c]
-        remote(blk, blk, s_y.at[0], x_recv.at[line, line_c], (g, i_y, c)).wait_recv()
-
-    @pl.when(c < C - 1)
-    def _():
-        right(c).start()
-
-    @pl.when(c > 0)
-    def _():
-        left(c).start()
-
-    over(c).start()
-    sib(0, c).start()
+        blk = piece(line, line_c, p)
+        return remote(blk, blk, s_sib.at[which, line_c, p], x_recv.at[line, line_c, p], (g, i_s, c))
+
+    def arrive(line, line_c, p):
+        blk = piece(line, line_c, p)
+        remote(blk, blk, s_y.at[0, p], x_recv.at[line, line_c, p], (g, i_y, c)).wait_recv()
+
+    for p in range(2):
+        @pl.when(c < C - 1)
+        def _():
+            right(c, p).start()
+
+        @pl.when(c > 0)
+        def _():
+            left(c, p).start()
+
+        over(c, p).start()
+        sib(0, c, p).start()
     coefs = []
     for k in range(1, E):
         o = (i + k) % E
@@ -103,6 +118,8 @@
         coefs.append(cp)
 
     loads[0].wait()
+    for ld in loads[1:]:
+        ld.start()
     CH = 16
 
     def mixing(step, carry):
@@ -128,58 +145,69 @@
     def mix_cross(src):
         return remote(mix.at[g, src], mix.at[g, src], g_send.at[src], g_recv.at[src], (1 - g, i, c))
 
-    for d in range(C - 1, 0, -1):
-        @pl.when(c - d >= 0)
-        def _():
-            mix_to(c - d).start()
-
-        @pl.when(c + d < C)
-        def _():
-            mix_to(c + d).start()
-
+    def mix_start(d):
+        for s in (-d, d):
+            dest = c + s
+
+            @pl.when((dest >= 0) & (dest < C))
+            def _():
+                mix_to(dest).start()
+
+    def mix_pass(d):
+        for s in (-d, d):
+            src = c + s
+
+            @pl.when((src >= 0) & (src < C))
+            def _():
+                mix_from(src).wait_recv()
+                mix_cross(src).start()
+
+    mix_start(1)
     mix[g, c] = mstage[c]
     mix_cross(c).start()
 
     def arrive_b(d):
-        for s in ((0,) if d == 0 else (-d, d)):
-            src = c + s
-
-            @pl.when((src >= 0) & (src < C))
-            def _():
-                arrive(i_y, src)
-                sib(1, src).start()
+        for p in range(2):
+            for s in ((0,) if d == 0 else (-d, d)):
+                src = c + s
+
+                @pl.when((src >= 0) & (src < C))
+                def _():
+                    arrive(i_y, src, p)
+                    sib(1, src, p).start()
 
     for d in range(1, C):
-        @pl.when(c - d >= 0)
-        def _():
-            arrive(i, c - d)
-
-            @pl.when(c < C - 1)
-            def _():
-                right(c - d).start()
-
-            over(c - d).start()
-            sib(0, c - d).start()
-
-        @pl.when(c + d < C)
-        def _():
-            arrive(i, c + d)
-
-            @pl.when(c > 0)
-            def _():
-                left(c + d).start()
-
-            over(c + d).start()
-            sib(0, c + d).start()
-
+        for p in range(2):
+            @pl.when(c - d >= 0)
+            def _():
+                arrive(i, c - d, p)
+
+                @pl.when(c < C - 1)
+                def _():
+                    right(c - d, p).start()
+
+                over(c - d, p).start()
+                sib(0, c - d, p).start()
+
+            @pl.when(c + d < C)
+            def _():
+                arrive(i, c + d, p)
+
+                @pl.when(c > 0)
+                def _():
+                    left(c + d, p).start()
+
+                over(c + d, p).start()
+                sib(0, c + d, p).start()
+
+        if d < C - 1:
+            mix_start(d + 1)
         arrive_b(d - 1)
-        for s in (-d, d):
-            src = c + s
-
-            @pl.when((src >= 0) & (src < C))
-            def _():
-                mix_from(src).wait_recv()
-                mix_cross(src).start()
+        if d > 1:
+            mix_pass(d - 1)
+
+    arrive_b(C - 1)
+    mix_pass(C - 1)
 
     loads[1].wait()
 
@@ -189,11 +217,10 @@
         low[line, 1] = dot(rows, fin[1]).astype(BF16)
 
     project(i)
-    arrive_b(C - 1)
     for k in range(C):
-        arrive(i_s, k)
-    for k in range(C):
-        arrive(i_d, k)
+        for p in range(2):
+            arrive(i_s, k, p)
+            arrive(i_d, k, p)
     lax.fori_loop(1, E, lambda k, carry: (project((i + k) % E), carry)[1], 0)
     for k in range(C):
         remote(mix.at[g, k], mix.at[1 - g, k], g_send.at[k], g_recv.at[k], (1 - g, i, c)).wait_recv()
@@ -223,10 +250,15 @@
     for k in list(range(1, E)) + [0]:
         line = (i + k) % E
         expert(k, 0)
-        for m in range(C):
-            dest = (c + m) % C
-            if k or m:
-                z_to(line, dest).start()
+        for m in range(C - 1, -1, -1):
+            for s in ((0,) if m == 0 else (-m, m)):
+                if k == 0 and m == 0:
+                    continue
+                dest = c + s
+
+                @pl.when((dest >= 0) & (dest < C))
+                def _():
+                    z_to(line, dest).start()
     zall[me] = zstage[i]
 
     for k in range(1, E):
@@ -255,42 +287,44 @@
 
         lax.fori_loop(0, C * T // 16, combine, 0)
 
-    step_w = 256
-    for n in range(OW // step_w):
-        cols = slice(n * step_w, (n + 1) * step_w)
-        block = dot(spread[...], bout[:, cols]).astype(BF16)
-        ostage[:, :, cols] = block.reshape(C, T, step_w)
-
-    def o_to(dest):
-        return remote(ostage.at[dest], oall.at[c], o_send.at[dest], o_recv.at[c], (g, i, dest))
-
-    for k in range(1, C):
-        o_to((c + k) % C).start()
-    oall[c] = ostage[c]
-    for k in range(1, C):
-        o = (c + k) % C
-        remote(ostage.at[o], oall.at[o], o_send.at[o], o_recv.at[o], (g, i, o)).wait_recv()
+    steps = o_send.shape[1]
+    step_w = OW // steps
+
+    def o_copy(n, dest, src):
+        return remote(ostage.at[n, dest], oall.at[n, src], o_send.at[dest, n], o_recv.at[src, n], (g, i, dest))
+
+    for n in range(steps):
+        block = dot(spread[...], bout[:, n * step_w : (n + 1) * step_w]).astype(BF16)
+        ostage[n] = block.reshape(C, T, step_w)
+        for k in range(1, C):
+            o_copy(n, (c + k) % C, c).start()
+        oall[n, c] = ostage[n, c]
+    for n in range(steps):
+        for k in range(1, C):
+            o_copy(n, (c + k) % C, (c + k) % C).wait_recv()
+        for k in range(C):
+            out_ref[:, k * OW + n * step_w : k * OW + (n + 1) * step_w] = oall[n, k]
+
     for k in range(C):
-        out_ref[:, k * OW : (k + 1) * OW] = oall[k]
-
-    for k in range(C):
-        @pl.when((c < C - 1) & (k <= c))
-        def _():
-            right(k).wait_send()
-
-        @pl.when((c > 0) & (k >= c))
-        def _():
-            left(k).wait_send()
-
-        over(k).wait_send()
-        sib(0, k).wait_send()
-        sib(1, k).wait_send()
+        for p in range(2):
+            @pl.when((c < C - 1) & (k <= c))
+            def _():
+                right(k, p).wait_send()
+
+            @pl.when((c > 0) & (k >= c))
+            def _():
+                left(k, p).wait_send()
+
+            over(k, p).wait_send()
+            sib(0, k, p).wait_send()
+            sib(1, k, p).wait_send()
         mix_cross(k).wait_send()
     for cp in coefs:
         cp.wait_send()
     for k in range(1, C):
         mix_to((c + k) % C).wait_send()
-        o_to((c + k) % C).wait_send()
+        for n in range(steps):
+            o_copy(n, (c + k) % C, c).wait_send()
     for k in range(E):
         for m in range(C):
             if k or m:
@@ -309,9 +343,13 @@
     return pl.pallas_call(
         functools.partial(fused, E, C),
         out_shape=jax.ShapeDtypeStruct((T, D), BF16),
-        in_specs=[vm, vm, pl.BlockSpec(memory_space=pltpu.SMEM), vm, vm, anym, anym, anym, anym],
+        in_specs=[anym] * 8,
         out_specs=vm,
         scratch_shapes=[
+            pltpu.VMEM((expert_ids.shape[1], T), jnp.int32),
+            pltpu.VMEM((expert_ids.shape[1], T), BF16),
+            pltpu.SMEM(mix_coef.shape, F32),
+            pltpu.VMEM(mix_coef.shape, F32),
             pltpu.VMEM((E, C, T, D + 128), BF16),
             pltpu.VMEM((2, D, R), BF16),
             pltpu.VMEM((FFU, R), BF16),
@@ -325,17 +363,17 @@
             pltpu.VMEM((E, C * T, R), BF16),
             pltpu.VMEM((E * C, C * T, R), BF16),
             pltpu.VMEM((C * T, J * R), BF16),
-            pltpu.VMEM((C, T, OW), BF16),
-            pltpu.VMEM((C, T, OW), BF16),
-            dma((4,)), dma, dma((C,)), dma((C,)), dma((C,)), dma((2, C)), dma((E, C)),
+            pltpu.VMEM((4, C, T, OW // 4), BF16),
+            pltpu.VMEM((4, C, T, OW // 4), BF16),
+            dma((5,)), dma((4,)), dma, dma((C, 2)), dma((C, 2)), dma((C, 2)), dma((2, C, 2)), dma((E, C, 2)),
             dma((C,)), dma((C,)), dma((C,)), dma((C,)),
-            dma((E,)), dma((E,)), dma((E, C)), dma((E * C,)), dma((C,)), dma((C,)),
+            dma((E,)), dma((E,)), dma((E, C)), dma((E * C,)), dma((C, 4)), dma((C, 4)),
         ],
         compiler_params=pltpu.CompilerParams(
-            collective_id=0, has_side_effects=True, vmem_limit_bytes=48 * 1024 * 1024
+            collective_id=0, has_side_effects=True, vmem_limit_bytes=62 * 1024 * 1024
         ),
     )(
-        expert_ids, gate_weights, mix_coef, mix_coef, tokens, factor_in, factor_out, basis_in,
+        expert_ids.T, gate_weights.T, mix_coef, tokens, factor_in, factor_out, basis_in,
         basis_out.reshape(J * R, OW),
     )
 

time: 59.7 us -> 53.9 us (0.903)
  local copies, waits for them, and re-layouts: 6.65 us -> 1.57 us
  Pallas kernels: 52.7 us -> 52.1 us
    unnamed x11 -> x1, local copies, waits for them, and re-layouts: 6.65 us -> 1.57 us
where the time goes in v3:
time: 53.9 us; the launch traced here: 53.7 us
  Pallas kernels  52.1 us (97%)
  local copies, waits for them, and re-layouts  1.57 us (3%)
    pallas_call x1, Pallas kernels, shards_kernel(): pl.pallas_call(functools.partial(fused, E, C), out_shape=jax.ShapeDtypeSt...  52.1 us
    unnamed x1, local copies, waits for them, and re-layouts  1.57 us

profile of v3, /device:TPU:0, one launch (start us, length us, event | category | flops | bytes accessed | tf_op | source)
XLA Modules:
  0.0 53.7 jit_solution(7553247655389919285)
XLA Ops:
  0.0 52.1 %shard_map.82 = bf16[16,4096]{1,0:T(8,128)(2,1)} custom-call(s32[8,16]{1,0:T(8,128)} %bitcast.4, bf16[8,16]{1,0:T(8,128)(2,1)} %bitcast.5, f32[4,2,16]{2,1,0:T(2,128)} %coef_hbm.1, bf16[16,4096]{1,0:T(8,128)(2,1)} %tok_hbm.1, bf16[1,2,4096,256]{3,2,1,0:T(8,128)(2,1)} %fin_hbm.1, bf16[1,768,256]{2,1,0:T(8,128)(2,1)} %fout_hbm.1, ...), custom_call_target="tpu_custom_call" | custom-call | tf_op jit(solution)/shard_map/pallas_call | solution.py:343
  52.1 1.6 %copy.10 = bf16[16,4096]{1,0:T(8,128)(2,1)} copy(bf16[16,4096]{1,0:T(8,128)(2,1)} %shard_map.82) | data formatting | bytes 262144

commit v4 on v3

--- a/solution.py
+++ b/solution.py
@@ -217,11 +217,12 @@
         low[line, 1] = dot(rows, fin[1]).astype(BF16)
 
     project(i)
-    for k in range(C):
-        for p in range(2):
-            arrive(i_s, k, p)
-            arrive(i_d, k, p)
-    lax.fori_loop(1, E, lambda k, carry: (project((i + k) % E), carry)[1], 0)
+    project(i_y)
+    for line in (i_s, i_d):
+        for k in range(C):
+            for p in range(2):
+                arrive(line, k, p)
+        project(line)
     for k in range(C):
         remote(mix.at[g, k], mix.at[1 - g, k], g_send.at[k], g_recv.at[k], (1 - g, i, c)).wait_recv()
     loads[2].wait()

time: 53.9 us -> 53 us (0.983)
  Pallas kernels: 52.1 us -> 51.3 us
    pallas_call x1, Pallas kernels: 52.1 us -> 51.3 us  [shards_kernel(): pl.pallas_call(functools.partial(fused, E, C), out_shape=jax.ShapeDtypeSt...]
where the time goes in v4:
time: 53 us; the launch traced here: 52.8 us
  Pallas kernels  51.3 us (97%)
  local copies, waits for them, and re-layouts  1.57 us (3%)
    pallas_call x1, Pallas kernels, shards_kernel(): pl.pallas_call(functools.partial(fused, E, C), out_shape=jax.ShapeDtypeSt...  51.3 us
    unnamed x1, local copies, waits for them, and re-layouts  1.57 us

profile of v4, /device:TPU:0, one launch (start us, length us, event | category | flops | bytes accessed | tf_op | source)
XLA Modules:
  0.0 52.8 jit_solution(15100392976702456037)
XLA Ops:
  0.0 51.3 %shard_map.82 = bf16[16,4096]{1,0:T(8,128)(2,1)} custom-call(s32[8,16]{1,0:T(8,128)} %bitcast.4, bf16[8,16]{1,0:T(8,128)(2,1)} %bitcast.5, f32[4,2,16]{2,1,0:T(2,128)} %coef_hbm.1, bf16[16,4096]{1,0:T(8,128)(2,1)} %tok_hbm.1, bf16[1,2,4096,256]{3,2,1,0:T(8,128)(2,1)} %fin_hbm.1, bf16[1,768,256]{2,1,0:T(8,128)(2,1)} %fout_hbm.1, ...), custom_call_target="tpu_custom_call" | custom-call | tf_op jit(solution)/shard_map/pallas_call | solution.py:344
  51.3 1.6 %copy.10 = bf16[16,4096]{1,0:T(8,128)(2,1)} copy(bf16[16,4096]{1,0:T(8,128)(2,1)} %shard_map.82) | data formatting | bytes 262144
